TPU v7x, 768 devices: a whole 4x8x12 slice. The times are simulated.
768 devices in a mesh: fsdp: 192 (over y, z_lo, x), tp: 4 (over z_hi, core).
Axes of the slice: x: 4, y: 8, z: 12 (z_hi: 2, z_lo: 6; z = z_hi * 6 + z_lo), core: 2. Of those that a mesh axis runs over, the one named last changes fastest.
Arguments:
- tokens: bfloat16 [49152, 2048], P(('fsdp', 'tp')), may hold values from -6 to 6
- norm_gain: float32 [2048], replicated, may hold values from 0.5 to 1.5
- in_weight: bfloat16 [2048, 6144], P(None, ('fsdp', 'tp')), may hold values from -0.125 to 0.125
- filter_taps: float32 [128, 128], P('tp'), may hold values from -0.5 to 0.5
- skip_gain: float32 [2048], P('tp'), may hold values from 0.5 to 2
Outputs:
- gated: bfloat16 [49152, 2048], P('fsdp', 'tp')
All inputs are finite; a program needn't handle non-finite values.
Results may differ from a plain program's by a relative error of at most 0.007.
Values may be sent and summed in bfloat16 or wider, within the bound.
A program may use at most 32 MiB of HBM per device.

v0:
```python
import jax
import jax.numpy as jnp
from jax import lax
from jax.sharding import PartitionSpec as P


def passed_along(block, axis, distance):
    devices = range(lax.axis_size(axis))
    route = [(i - distance, i) for i in devices if i - distance in devices]
    return lax.ppermute(block, axis, route)


def causal_blocks(extended, filter_taps):
    tap_count = filter_taps.shape[1]
    row_count = extended.shape[0] - tap_count
    channels = extended.shape[1]
    groups = filter_taps.shape[0]
    group_width = channels // groups
    offset = jnp.arange(tap_count)[:, None] - jnp.arange(tap_count)[None, :]
    near_taps = jnp.where(offset >= 0, filter_taps[:, jnp.clip(offset, 0, tap_count - 1)], 0.0)
    far_taps = jnp.where(
        offset < 0, filter_taps[:, jnp.clip(offset + tap_count, 0, tap_count - 1)], 0.0
    )
    widened = extended.astype(jnp.float32)
    block_shape = (row_count // tap_count, tap_count, groups, group_width)
    current = widened[tap_count:].reshape(block_shape)
    earlier = widened[:-tap_count].reshape(block_shape)
    result = jnp.einsum("gij,bjgc->bigc", near_taps, current, precision=lax.Precision.HIGHEST)
    result = result + jnp.einsum(
        "gij,bjgc->bigc", far_taps, earlier, precision=lax.Precision.HIGHEST
    )
    return result.reshape(row_count, channels)


def shards(tokens, norm_gain, in_weight, filter_taps, skip_gain):
    tap_count = filter_taps.shape[1]
    features = tokens.astype(jnp.float32)
    power = jnp.mean(features * features, axis=1, keepdims=True)
    normed = (features * lax.rsqrt(power + 1e-06) * norm_gain).astype(jnp.bfloat16)
    slab_rows = lax.all_gather(normed, "tp", axis=0, tiled=True)
    full_weight = lax.all_gather(in_weight, "fsdp", axis=1, tiled=True)
    proj_all = jnp.dot(slab_rows, full_weight, preferred_element_type=jnp.float32)
    channels = proj_all.shape[1] // 3
    mixed = (proj_all[:, channels : 2 * channels] * proj_all[:, 2 * channels :]).astype(
        jnp.bfloat16
    )
    mixed_edge = passed_along(mixed[-tap_count:], "fsdp", 1)
    query = proj_all[:, :channels]
    extended = jnp.concatenate([mixed_edge, mixed], axis=0)
    conv = causal_blocks(extended, filter_taps)
    return (query * (conv + skip_gain * mixed.astype(jnp.float32))).astype(jnp.bfloat16)


def solution(mesh):
    return jax.shard_map(
        shards,
        mesh=mesh,
        in_specs=(P(("fsdp", "tp"), None), P(), P(None, ("fsdp", "tp")), P("tp", None), P("tp")),
        out_specs=P("fsdp", "tp"),
        check_vma=False,
    )
```

profile of v0, /device:TPU:2, one launch (start us, length us, event | category | flops | bytes accessed | tf_op | source)
XLA Modules:
  0.0 1493.3 jit_solution(4764889936750425105)
XLA Ops:
  6.5 0.0 all-gather.3.cloned.1.call-start
  6.5 1.1 fusion.16
  7.7 1.8 fusion.18
  9.4 0.0 all-gather.3.cloned.1.call-update
  9.5 0.0 all-gather.5.cloned.1.call-start
  9.5 0.7 all-gather.5.cloned.1.call-update
  10.3 0.0 copy-start.3
  10.3 52.1 %all-gather.3.cloned.1.call-done = bf16[256,2048]{1,0:T(8,128)(2,1)} async-done(((bf16[64,2048]{1,0:T(8,128)(2,1)}), bf16[256,2048]{1,0:T(8,128)(2,1)}) %all-gather.3.cloned.1.call-update) | async-done | bytes 1048592 | tf_op jit(solution)/shard_map/all_gather | solution.py:40
  62.4 1289.6 %all-gather.5.cloned.1.call-done = bf16[2048,1536]{0,1:T(8,128)(2,1)} async-done(((bf16[2048,8]{0,1:T(8,128)(2,1)}), bf16[2048,1536]{0,1:T(8,128)(2,1)}) %all-gather.5.cloned.1.call-update) | async-done | bytes 6291472 | tf_op jit(solution)/shard_map/all_gather | solution.py:41
  1352.0 4.9 fusion.31
  1356.9 0.0 copy-start.1
  1356.9 0.1 fusion.19
  1357.0 1.9 collective-permute-start
  1359.0 0.0 copy-done.1
  1359.0 0.0 copy-done.3
  1359.0 0.1 copy.14
  1359.1 54.5 %gather_fusion.1 = f32[16384,32]{1,0:T(8,128)} fusion(f32[32,128]{0,1:T(8,128)S(1)} %copy.14, s32[16384]{0:T(1024)S(1)} %fusion.26), kind=kCustom, calls=%fused_computation.1 | custom fusion | bytes 4259840 | tf_op jit(solution)/shard_map/gather | solution.py:22
  1413.6 5.5 copy.19
  1419.1 54.5 %gather_fusion = f32[16384,32]{1,0:T(8,128)} fusion(f32[32,128]{0,1:T(8,128)S(1)} %copy.14, s32[16384]{0:T(1024)S(1)} %fusion.24), kind=kCustom, calls=%fused_computation | custom fusion | bytes 4259840 | tf_op jit(solution)/shard_map/gather | solution.py:20
  1473.6 6.5 copy.15
  1480.1 0.1 copy.13
  1480.3 0.1 reshape.69
  1480.3 0.0 collective-permute-done
  1480.4 0.1 copy.17
  1480.5 0.1 reshape.70
  1480.6 1.8 fusion
  1482.3 1.8 fusion.9
  1484.1 0.0 copy-start.4
  1484.1 0.3 copy.21
  1484.4 0.2 copy.22
  1484.7 0.9 copy-done.2
  1485.5 0.9 fusion.20
  (12 shorter events, 0.2 us)
Async XLA Ops:
  6.5 55.8 %all-gather.3.cloned.1.call-start = ((), (), s32[]{:S(2)}) async-start(), calls=%async_computation | async-start | bytes 1310720 | tf_op jit(solution)/shard_map/all_gather | solution.py:40
  9.5 1342.5 %all-gather.5.cloned.1.call-start = ((), (), s32[]{:S(2)}) async-start(), calls=%async_computation.1 | async-start | bytes 6324224 | tf_op jit(solution)/shard_map/all_gather | solution.py:41
  10.3 1348.7 %copy-start.3 = (f32[32,128]{1,0:T(8,128)S(1)}, f32[32,128]{1,0:T(8,128)}, u32[]{:S(2)}) copy-start(f32[32,128]{1,0:T(8,128)} %param.8) | copy-start | bytes 49156
  1356.9 2.0 copy-start.1
  1357.0 123.3 %collective-permute-start = (bf16[128,512]{1,0:T(8,128)(2,1)S(1)}, bf16[128,512]{1,0:T(8,128)(2,1)S(1)}, u32[]{:S(2)}, u32[]{:S(2)}) collective-permute-start(bf16[128,512]{1,0:T(8,128)(2,1)S(1)} %slice.28), channel_id=1, source_target_pairs={{0,4},{4,8},{8,12},{12,16},{16,20},{20,24},{24,28},{28,32},{32,36}... | collective-permute-start | bytes 393224 | tf_op jit(solution)/shard_map/ppermute | solution.py:10
  1480.6 1.8 copy-start
  1484.1 1.4 copy-start.2
  1484.1 1.4 copy-start.4
Sparse Core Ops, SparseCore 0:
  9.8 52.5 all-gather.2
  64.8 1287.1 all-gather.4
where the time goes:
time: 1490 us
  waiting for transfers between devices  1340 us (90%)
  local copies, waits for them, and re-layouts  123 us (8%)
    all_gather x1, waiting for transfers between devices, shards(): full_weight = lax.all_gather(in_weight, 'fsdp', axis=1, tiled=True)  1290 us
    gather x2, local copies, waits for them, and re-layouts, causal_blocks(): filter_taps[:, jnp.clip(offset, 0, tap_count - 1)]  61 us
    gather x2, local copies, waits for them, and re-layouts, causal_blocks(): filter_taps[:, jnp.clip(offset + tap_count, 0, tap_count - 1)]  60 us
    all_gather x1, waiting for transfers between devices, shards(): slab_rows = lax.all_gather(normed, 'tp', axis=0, tiled=True)  52.1 us
  transfers between devices with their start and end apart: 3, of which 2 were waited for; matrix products, arithmetic and copies ran while one was open for 8% of the time, Pallas kernels for 0%

commit v1 on v0

v1 whole, which is shorter than its diff:
```python
import functools

import jax
import jax.numpy as jnp
from jax import lax
from jax.experimental import pallas as pl
from jax.experimental.pallas import tpu as pltpu
from jax.sharding import PartitionSpec as P

MESH = pl.DeviceIdType.MESH
NX, NY, NZ = 4, 8, 6
KC = 4
NT = (((1,), (1,)), ((), ()))


def reach(direction, d):
    return (4 if d < 3 else 3) if direction > 0 else (3 if d < 3 else 4)


def channels():
    names = [("wz", d) for d in range(1, NZ)]
    for d in range(NZ):
        for direction in (1, -1):
            names += [("wy", direction, s, d) for s in range(1, reach(direction, d) + 1)]
    names += [("ox", k) for k in range(1, NX)] + [("os", k) for k in range(NX)]
    for kc in range(KC):
        names += [("cr", kc)]
        names += [("cx", kc, k) for k in range(1, NX)] + [("cs", kc, k) for k in range(NX)]
    names += [("edge",)] + [("out", k) for k in range(1, NX)]
    return {name: i for i, name in enumerate(names)}


CH = channels()


def kernel(
    tokens_ref, gain_ref, w_ref, taps_ref, skip_ref, out_ref,
    tb, wb, acc, toep, skip_b, qb, mx, edge_out, edge_in, send_out, got, ssem, rsem,
):
    f = lax.axis_index("fsdp")
    t = lax.axis_index("tp")
    x = f % NX
    g = f // NX
    zl = g % NZ
    y = g // NZ
    h = t // 2
    c = t % 2
    taps = taps_ref.shape[1]
    chunk = tb.shape[-1]

    def dev(y_, zl_, x_, h_, c_):
        return ((y_ * NZ + zl_) * NX + x_, h_ * 2 + c_)

    def zpeer(d):
        return dev(y, (zl + d) % NZ, x, h, c)

    def ypeer(d):
        return dev((y + d + NY) % NY, zl, x, h, c)

    def xpeer(k):
        return dev(y, zl, (x + k) % NX, h, c)

    sibling = dev(y, zl, x, h, 1 - c)
    partner = dev(y, zl, x, 1 - h, c)
    g_next = (g + 1) % (NY * NZ)
    g_prev = (g + NY * NZ - 1) % (NY * NZ)
    after = dev(g_next // NZ, g_next % NZ, x, h, c)
    before = dev(g_prev // NZ, g_prev % NZ, x, h, c)

    sends = []

    def copy(name, src, dst, to):
        return pltpu.make_async_remote_copy(
            src_ref=src, dst_ref=dst, send_sem=ssem.at[CH[name]], recv_sem=rsem.at[CH[name]],
            device_id=to, device_id_type=MESH,
        )

    def send(name, src, dst, to):
        one = copy(name, src, dst, to)
        one.start()
        sends.append(one)

    def arrived(name, dst):
        copy(name, dst, dst, sibling).wait_recv()

    features = tokens_ref[...].astype(jnp.float32)
    power = jnp.mean(features * features, axis=1, keepdims=True)
    normed = (features * lax.rsqrt(power + 1e-06) * gain_ref[...]).astype(jnp.bfloat16)
    for kc in range(KC):
        tb[kc, 0, x, c] = normed[:, kc * chunk : (kc + 1) * chunk]
    wb[g] = w_ref[...]

    barrier = pltpu.get_barrier_semaphore()
    greet = [zpeer(d) for d in range(1, NZ)] + [ypeer(1), ypeer(-1)]
    greet += [xpeer(k) for k in range(1, NX)] + [sibling, partner, after, before]
    for peer in greet:
        pl.semaphore_signal(barrier, inc=1, device_id=peer, device_id_type=MESH)
    pl.semaphore_wait(barrier, len(greet))

    def column(d):
        return (zl + NZ - d) % NZ

    def block(y_, d):
        return wb.at[y_ * NZ + column(d)]

    def pass_on(direction, s, d):
        if s <= reach(direction, d):
            here = block((y - direction * (s - 1) + NY) % NY, d)
            send(("wy", direction, s, d), here, here, ypeer(direction))

    def on_wz(d):
        arrived(("wz", d), block(y, d))
        pass_on(1, 1, d)
        pass_on(-1, 1, d)

    def on_wy(direction, s, d):
        arrived(("wy", direction, s, d), block((y - direction * s + NY) % NY, d))
        pass_on(direction, s + 1, d)

    def own_piece(k, c_):
        return tb.at[:, 0, (x + NX - k) % NX, c_]

    def far_piece(kc, k, c_):
        return tb.at[kc, 1, (x + NX - k) % NX, c_]

    def on_ox(k):
        piece = own_piece(k, c)
        arrived(("ox", k), piece)
        send(("os", k), piece, piece, sibling)

    def on_cr(kc):
        piece = far_piece(kc, 0, c)
        arrived(("cr", kc), piece)
        for k in (2, 1, 3):
            send(("cx", kc, k), piece, piece, xpeer(k))
        send(("cs", kc, 0), piece, piece, sibling)

    def on_cx(kc, k):
        piece = far_piece(kc, k, c)
        arrived(("cx", kc, k), piece)
        send(("cs", kc, k), piece, piece, sibling)

    here = block(y, 0)
    for d in range(1, NZ):
        send(("wz", d), here, here, zpeer(d))
    pass_on(1, 1, 0)
    pass_on(-1, 1, 0)
    for kc in range(KC):
        send(("cr", kc), tb.at[kc, 0, x, c], tb.at[kc, 1, x, c], partner)
    for k in (2, 1, 3):
        send(("ox", k), own_piece(0, c), own_piece(0, c), xpeer(k))
    send(("os", 0), own_piece(0, c), own_piece(0, c), sibling)

    row_at = lax.broadcasted_iota(jnp.int32, (taps, taps), 0)
    lane_at = lax.broadcasted_iota(jnp.int32, (taps, taps), 1)

    def table(j):
        one = taps_ref[pl.ds(2 * j + x // 2, 1), :]
        rolled = pltpu.roll(jnp.broadcast_to(one, (taps, taps)), 0, 1, stride=1, stride_axis=0)
        toep[j, 0:taps] = jnp.where(lane_at < row_at, rolled, 0.0).astype(jnp.bfloat16)
        toep[j, taps : 2 * taps] = jnp.where(lane_at >= row_at, rolled, 0.0).astype(jnp.bfloat16)

    def skips():
        wide = jnp.broadcast_to(skip_ref[...], (128, skip_ref.shape[1]))
        skip_b[...] = wide.T.reshape(skip_b.shape)

    events = []
    for d in range(1, NZ):
        events.append((1.5 + 1.1 * d, lambda d=d: on_wz(d)))
    for d in range(NZ):
        for direction in (1, -1):
            for s in range(1, reach(direction, d) + 1):
                when = 1.9 * s + 1.1 * d + (1.5 if d else 0.0) + 0.01 * direction
                events.append((when, lambda a=direction, s=s, d=d: on_wy(a, s, d)))
    for k in range(1, NX):
        events.append((11.0 if k == 2 else 8.0, lambda k=k: on_ox(k)))
    for kc in range(KC):
        base = 6.0 + 4.0 * (kc + 1)
        events.append((base, lambda kc=kc: on_cr(kc)))
        for k in range(1, NX):
            events.append((base + (4.0 if k == 2 else 3.5), lambda kc=kc, k=k: on_cx(kc, k)))

    def project(kc, which):
        rows = tb[kc, which].reshape(-1, chunk)
        part = wb[:, :, kc * chunk : (kc + 1) * chunk].reshape(-1, chunk)
        return lax.dot_general(part, rows, NT, preferred_element_type=jnp.float32)

    def own_half():
        for k in range(NX):
            arrived(("os", k), own_piece(k, 1 - c))
        acc[...] = project(0, 0)
        for kc in range(1, KC):
            acc[...] += project(kc, 0)
        spread(h)

    def other_half(kc):
        for k in range(NX):
            arrived(("cs", kc, k), far_piece(kc, k, 1 - c))
        if kc == 0:
            acc[...] = project(kc, 1)
        else:
            acc[...] += project(kc, 1)

    def spread(half):
        for slab in range(NX):
            part = acc[:, slab * 128 : (slab + 1) * 128]
            qb[2 * slab + half] = part[0:128]
            mixed = (part[128:256] * part[256:384]).astype(jnp.bfloat16)
            mx[1 + 2 * slab + half] = mixed.astype(jnp.float32)

    last_w = max(when for when, _ in events if when < 17.0)
    events.append((17.5, own_half))
    for kc in range(KC):
        events.append((max(17.6 + 0.01 * kc, 6.0 + 4.0 * (kc + 1) + 5.0), lambda kc=kc: other_half(kc)))
    events.append((2.1, skips))
    for j in range(16):
        events.append((2.2 + 0.5 * j, lambda j=j: table(j)))
    for _, event in sorted(events, key=lambda e: e[0]):
        event()

    spread(1 - h)
    edge_out[...] = mx[2 * NX].astype(jnp.bfloat16)
    send(("edge",), edge_out, edge_in, after)
    arrived(("edge",), edge_in)
    before_first = edge_in[...].astype(jnp.float32)
    mx[0] = jnp.where(g == 0, jnp.zeros_like(before_first), before_first)

    blocks = 2 * NX
    for j in range(16):
        rows = slice(8 * j, 8 * j + 8)
        now = mx[1 : 1 + blocks, rows, :]
        window = jnp.concatenate([mx[0:blocks, rows, :], now], axis=2)
        window = window.reshape(8 * blocks, 2 * taps).astype(jnp.bfloat16)
        conv = jnp.dot(window, toep[j], preferred_element_type=jnp.float32)
        direct = skip_b[j, pl.ds(x, 1)] * now
        gated = qb[:, rows, :] * (conv.reshape(blocks, 8, taps) + direct)
        gated = gated.reshape(NX, 2, 8, taps).astype(jnp.bfloat16)
        send_out[:, j, :, 0:taps] = gated[:, 0]
        send_out[:, j, :, taps : 2 * taps] = gated[:, 1]

    for k in (2, 1, 3):
        send(("out", k), send_out.at[(x + k) % NX], got.at[:, x], xpeer(k))
    got[:, x] = send_out[x]
    for k in range(1, NX):
        arrived(("out", k), got.at[:, (x + NX - k) % NX])
    out_ref[...] = got[...].astype(jnp.float32).reshape(out_ref.shape).astype(jnp.bfloat16)
    for one in sends:
        one.wait_send()


def shards(tokens, norm_gain, in_weight, filter_taps, skip_gain):
    rows, din = tokens.shape
    taps = filter_taps.shape[1]
    wide = skip_gain.shape[0]
    count = len(CH)
    vmem = pl.BlockSpec(memory_space=pltpu.VMEM)
    out = pl.pallas_call(
        kernel,
        out_shape=jax.ShapeDtypeStruct((wide, 4 * rows), jnp.bfloat16),
        in_specs=[vmem] * 5,
        out_specs=vmem,
        scratch_shapes=[
            pltpu.VMEM((KC, 2, NX, 2, rows, din // KC), jnp.bfloat16),
            pltpu.VMEM((NY * NZ, 8, din), jnp.bfloat16),
            pltpu.VMEM((8 * NY * NZ, NX * 2 * rows), jnp.float32),
            pltpu.VMEM((16, 2 * taps, taps), jnp.bfloat16),
            pltpu.VMEM((16, NX, 8, 128), jnp.float32),
            pltpu.VMEM((2 * NX, 128, 2 * rows), jnp.float32),
            pltpu.VMEM((2 * NX + 1, 128, 2 * rows), jnp.float32),
            pltpu.VMEM((128, 2 * rows), jnp.bfloat16),
            pltpu.VMEM((128, 2 * rows), jnp.bfloat16),
            pltpu.VMEM((NX, 16, 8, 4 * rows), jnp.bfloat16),
            pltpu.VMEM((16, NX, 8, 4 * rows), jnp.bfloat16),
            pltpu.SemaphoreType.DMA((count,)),
            pltpu.SemaphoreType.DMA((count,)),
        ],
        compiler_params=pltpu.CompilerParams(
            collective_id=0, has_side_effects=True, vmem_limit_bytes=40 * 2**20
        ),
    )(tokens, norm_gain.reshape(1, din), in_weight.T, filter_taps, skip_gain.reshape(1, wide))
    return out.T


def solution(mesh):
    return jax.shard_map(
        shards,
        mesh=mesh,
        in_specs=(P(("fsdp", "tp"), None), P(), P(None, ("fsdp", "tp")), P("tp", None), P("tp")),
        out_specs=P("fsdp", "tp"),
        check_vma=False,
    )
```

time: 1490 us -> 91.9 us (0.06)
  the two profiles are of different devices: /device:TPU:2 before, /device:TPU:1 now
where the time goes in v1:
time: 91.9 us; the launch traced here: 91.6 us
  Pallas kernels  86.9 us (95%)
  local copies, waits for them, and re-layouts  4.65 us (5%)
    pallas_call x1, Pallas kernels, shards(): pl.pallas_call(kernel, out_shape=jax.ShapeDtypeStruct((wide, 4 * rows), j...  86.9 us
    unnamed x10, local copies, waits for them, and re-layouts  3.8 us

profile of v1, /device:TPU:1, one launch (start us, length us, event | category | flops | bytes accessed | tf_op | source)
XLA Modules:
  0.0 91.6 jit_solution(994234422988679177)
XLA Ops:
  0.0 0.0 copy-start.4
  0.0 0.7 copy-done.4
  0.7 0.0 copy-start
  0.7 0.9 %copy-done = bf16[64,2048]{1,0:T(8,128)(2,1)S(1)} copy-done((bf16[64,2048]{1,0:T(8,128)(2,1)S(1)}, bf16[64,2048]{1,0:T(8,128)(2,1)}, u32[]{:S(2)}) %copy-start) | copy-done | bytes 262168
  1.6 0.0 copy-start.1
  1.6 0.8 copy-done.1
  2.4 0.0 copy-start.2
  2.4 0.7 copy-done.2
  3.1 0.0 copy-start.3
  3.1 0.7 copy-done.3
  3.8 86.9 %shard_map.55 = bf16[512,256]{1,0:T(8,128)(2,1)S(1)} custom-call(bf16[64,2048]{1,0:T(8,128)(2,1)S(1)} %copy-done, f32[1,2048]{1,0:T(1,128)S(1)} %bitcast.6, bf16[8,2048]{1,0:T(8,128)(2,1)S(1)} %bitcast.5, f32[32,128]{1,0:T(8,128)S(1)} %copy-done.2, f32[1,512]{1,0:T(1,128)S(1)} %bitcast.7), custom_call_target="tpu_custom_call" | custom-call | tf_op jit(solution)/shard_map/pallas_call | solution.py:257
  90.8 0.8 copy.6
Async XLA Ops:
  0.0 0.7 copy-start.4
  0.7 0.9 %copy-start = (bf16[64,2048]{1,0:T(8,128)(2,1)S(1)}, bf16[64,2048]{1,0:T(8,128)(2,1)}, u32[]{:S(2)}) copy-start(bf16[64,2048]{1,0:T(8,128)(2,1)} %tokens_ref.1) | copy-start | bytes 786436
  1.6 0.8 copy-start.1
  2.4 0.7 copy-start.2
  3.1 0.7 copy-start.3

commit v2 on v0

v2 whole, which is shorter than its diff:
```python
import functools

import jax
import jax.numpy as jnp
from jax import lax
from jax.experimental import pallas as pl
from jax.experimental.pallas import tpu as pltpu
from jax.sharding import PartitionSpec as P

MESH = pl.DeviceIdType.MESH
NX, NY, NZ = 4, 8, 6
KC = 8
Y_DEPTH = 4
CROSS_DEPTH = 2
GROUP = 2
OWN_AT = 7
OX_AT = 2
NT = (((1,), (1,)), ((), ()))


def reach(direction, d):
    return (4 if d < 3 else 3) if direction > 0 else (3 if d < 3 else 4)


def channels():
    names = [("wz", d) for d in range(NZ)] + [("ws", n) for n in range(NY * NZ)]
    for d in range(NZ):
        for direction in (1, -1):
            names += [("wy", direction, s, d) for s in range(1, reach(direction, d) + 1)]
    names += [("w0",), ("t0",)] + [("ox", k) for k in range(1, NX)] + [("os", k) for k in range(NX)]
    for kc in range(KC):
        names += [("cr", kc)]
        names += [("cx", kc, k) for k in range(1, NX)] + [("cs", kc, k) for k in range(NX)]
    names += [("edge",)] + [("out", k) for k in range(NX)]
    return {name: i for i, name in enumerate(names)}


CH = channels()


def y_order():
    first = [(1, 0), (2, 0), (3, 0), (1, 1), (1, 2), (4, 0), (1, 3), (1, 4), (1, 5)]
    return first + [(s, d) for s in (2, 3, 4) for d in range(1, NZ)]


def kernel(
    tokens_hbm, gain_hbm, w_hbm, taps_hbm, skip_hbm, out_ref,
    tokens_ref, gain_ref, taps_ref, skip_ref,
    tb, wb, acc, toep, skip_b, qb, mx, edge_out, edge_in, send_out, got, ssem, rsem, lsem, ready,
):
    f = lax.axis_index("fsdp")
    t = lax.axis_index("tp")
    x = f % NX
    g = f // NX
    zl = g % NZ
    y = g // NZ
    h = t // 2
    c = t % 2
    taps = taps_ref.shape[1]
    chunk = tb.shape[-1]

    def dev(y_, zl_, x_, h_, c_):
        return ((y_ * NZ + zl_) * NX + x_, h_ * 2 + c_)

    def zpeer(d):
        return dev(y, (zl + d) % NZ, x, h, c)

    def ypeer(d):
        return dev((y + d + NY) % NY, zl, x, h, c)

    def xpeer(k):
        return dev(y, zl, (x + k) % NX, h, c)

    sibling = dev(y, zl, x, h, 1 - c)
    partner = dev(y, zl, x, 1 - h, c)
    g_next = (g + 1) % (NY * NZ)
    g_prev = (g + NY * NZ - 1) % (NY * NZ)
    after = dev(g_next // NZ, g_next % NZ, x, h, c)
    before = dev(g_prev // NZ, g_prev % NZ, x, h, c)

    barrier = pltpu.get_barrier_semaphore()
    shared = [xpeer(k) for k in range(1, NX)] + [sibling]
    for_weight = [zpeer(d) for d in range(1, NZ)] + [ypeer(1), ypeer(-1)]

    def greet(peers):
        for peer in peers:
            pl.semaphore_signal(barrier, inc=1, device_id=peer, device_id_type=MESH)

    greet(shared + [before])

    @pl.when(c == 0)
    def _():
        greet(for_weight)

    @pl.when((c == 1) & (h == 0))
    def _():
        greet([partner])

    loads = [
        pltpu.make_async_copy(tokens_hbm, tokens_ref, lsem.at[0]),
        pltpu.make_async_copy(gain_hbm, gain_ref, lsem.at[1]),
        pltpu.make_async_copy(w_hbm, wb.at[g, c], lsem.at[2]),
        pltpu.make_async_copy(taps_hbm, taps_ref, lsem.at[3]),
        pltpu.make_async_copy(skip_hbm, skip_ref, lsem.at[4]),
    ]
    for load in loads:
        load.start()

    unsent = {}

    def copy(name, src, dst, to, at=None):
        return pltpu.make_async_remote_copy(
            src_ref=src, dst_ref=dst, send_sem=ssem.at[CH[name]],
            recv_sem=rsem.at[CH[name] if at is None else at], device_id=to, device_id_type=MESH,
        )

    def send(name, src, dst, to, at=None):
        one = copy(name, src, dst, to, at)
        one.start()
        unsent[name] = one

    def sent(name):
        if name in unsent:
            unsent.pop(name).wait_send()

    def all_sent():
        for name in list(unsent):
            sent(name)

    def arrived(name, dst, at=None):
        copy(name, dst, dst, sibling, at).wait_recv()

    loads[0].wait()
    loads[1].wait()
    features = tokens_ref[...].astype(jnp.float32)
    power = jnp.mean(features * features, axis=1, keepdims=True)
    normed = (features * lax.rsqrt(power + 1e-06) * gain_ref[...]).astype(jnp.bfloat16)
    for kc in range(KC):
        tb[kc, 0, x, c] = normed[:, kc * chunk : (kc + 1) * chunk]
    loads[2].wait()

    pl.semaphore_wait(barrier, len(shared) + 1 + jnp.where(c == 0, len(for_weight), h))

    row_at = lax.broadcasted_iota(jnp.int32, (taps, taps), 0)
    lane_at = lax.broadcasted_iota(jnp.int32, (taps, taps), 1)

    def tables():
        loads[3].wait()
        loads[4].wait()
        wide = jnp.broadcast_to(skip_ref[...], (128, skip_ref.shape[1]))
        skip_b[...] = wide.T.reshape(skip_b.shape)
        for j in range(16):
            one = taps_ref[pl.ds(2 * j + x // 2, 1), :]
            rolled = pltpu.roll(jnp.broadcast_to(one, (taps, taps)), 0, 1, stride=1, stride_axis=0)
            toep[j, 0:taps] = jnp.where(lane_at < row_at, rolled, 0.0).astype(jnp.bfloat16)
            toep[j, taps : 2 * taps] = jnp.where(lane_at >= row_at, rolled, 0.0).astype(jnp.bfloat16)

    def project(group, which):
        total = None
        for kc in range(group * GROUP, (group + 1) * GROUP):
            rows = tb[kc, which].reshape(-1, chunk)
            part = wb[:, c, :, kc * chunk : (kc + 1) * chunk].reshape(-1, chunk)
            term = lax.dot_general(part, rows, NT, preferred_element_type=jnp.float32)
            total = term if total is None else total + term
        return total

    def spread(half):
        for slab in range(NX):
            part = acc[:, slab * 128 : (slab + 1) * 128]
            qb[2 * slab + half] = part[0:128]
            mixed = (part[128:256] * part[256:384]).astype(jnp.bfloat16)
            mx[1 + 2 * slab + half] = mixed.astype(jnp.float32)

    def edge_copy():
        return copy(("edge",), edge_out, edge_in, after)

    def edge_send():
        edge_out[...] = mx[2 * NX].astype(jnp.bfloat16)
        edge_copy().start()

    def own_half():
        acc[...] = project(0, 0)
        for group in range(1, KC // GROUP):
            acc[...] += project(group, 0)
        spread(h)
        pl.when(h == 1)(edge_send)

    def column(d):
        return zl if d == 0 else jnp.where(d - 1 >= zl, d, d - 1)

    def place(y_, d):
        return (y_ + NY) % NY * NZ + column(d)

    def weight_role():
        def hand_on(n, key):
            send(("ws", key), wb.at[n, 1], wb.at[n, 1], sibling, CH[("ws", 0)] + n)

        keys = iter(range(NY * NZ))
        seen = set()

        def pass_on(direction, s, d):
            n = place(y - direction * (s - 1), d)
            if s > 1:
                arrived(("wy", direction, s - 1, d), wb.at[n])
            elif d and d not in seen:
                arrived(("wz", d), wb.at[n], CH[("wz", 0)] + column(d))
            if s <= reach(direction, d):
                at = order[direction].index((s, d))
                if at >= Y_DEPTH:
                    sent(("wy", direction, *order[direction][at - Y_DEPTH]))
                send(("wy", direction, s, d), wb.at[n], wb.at[n], ypeer(direction))
            if s > 1 or (d and d not in seen):
                hand_on(n, next(keys))
            seen.add(d)

        order = {a: [(s, d) for s, d in y_order() if s <= reach(a, d)] for a in (1, -1)}
        arrived(("w0",), wb.at[g, 1])
        own = wb.at[g]
        for d in range(1, NZ):
            send(("wz", d), own, own, zpeer(d), CH[("wz", 0)] + zl)
        pass_on(1, 1, 0)
        pass_on(-1, 1, 0)
        tables()
        for s, d in y_order()[1:] + [(5, d) for d in range(NZ)]:
            for direction in (1, -1):
                if s <= reach(direction, d) + 1:
                    pass_on(direction, s, d)

    def own_piece(k):
        return tb.at[:, 0, (x + NX - k) % NX]

    def far_piece(kc, k):
        return tb.at[kc, 1, (x + NX - k) % NX]

    def token_role():
        def on_ox(k):
            piece = own_piece(k)
            arrived(("ox", k), piece)
            send(("os", k), piece, piece, sibling)

        def cross(kc):
            if kc >= CROSS_DEPTH:
                sent(("cr", kc - CROSS_DEPTH))
            send(("cr", kc), tb.at[kc, 0, x], tb.at[kc, 1, x], partner)

        def on_cr(kc):
            piece = far_piece(kc, 0)
            arrived(("cr", kc), piece)
            for k in (2, 1, 3):
                send(("cx", kc, k), piece, piece, xpeer(k))
            send(("cs", kc, 0), piece, piece, sibling)

        def on_cx(kc, k):
            piece = far_piece(kc, k)
            arrived(("cx", kc, k), piece)
            send(("cs", kc, k), piece, piece, sibling)

        arrived(("t0",), tb.at[:, 0, x, 0])
        for k in (2, 1, 3):
            send(("ox", k), own_piece(0), own_piece(0), xpeer(k))

        @pl.when(h == 0)
        def _():
            pl.semaphore_wait(ready, 1)

        tables()
        for kc in range(CROSS_DEPTH):
            cross(kc)
        for kc in range(KC):
            on_cr(kc)
            if kc + CROSS_DEPTH < KC:
                cross(kc + CROSS_DEPTH)
            if kc >= 1:
                for k in (1, 3, 2):
                    on_cx(kc - 1, k)
            if kc == OWN_AT:
                for d in range(NY * NZ - 1):
                    n = jnp.where(d >= g, d + 1, d)
                    arrived(("ws", 0), wb.at[n, 1], CH[("ws", 0)] + n)
                own_half()
            if kc == OX_AT:
                for k in (1, 3, 2):
                    on_ox(k)
        for k in (1, 3, 2):
            on_cx(KC - 1, k)

    @pl.when((c == 1) & (h == 1))
    def _():
        pl.semaphore_signal(ready, inc=1, device_id=partner, device_id_type=MESH)

    @pl.when(c == 0)
    def _():
        send(("t0",), tb.at[:, 0, x, 0], tb.at[:, 0, x, 0], sibling)
        weight_role()
        arrived(("os", 0), tb.at[:, 0, x, 1])
        for k in range(1, NX):
            arrived(("os", k), own_piece(k))
        all_sent()
        own_half()

    @pl.when(c == 1)
    def _():
        send(("w0",), wb.at[g, 1], wb.at[g, 1], sibling)
        send(("os", 0), tb.at[:, 0, x, 1], tb.at[:, 0, x, 1], sibling)
        token_role()
        all_sent()

    for group in range(KC // GROUP):
        @pl.when(c == 0)
        def _(group=group):
            for kc in range(group * GROUP, (group + 1) * GROUP):
                for k in range(NX):
                    arrived(("cs", kc, k), far_piece(kc, k))

        if group == 0:
            acc[...] = project(group, 1)
        else:
            acc[...] += project(group, 1)
    spread(1 - h)

    pl.when(h == 0)(edge_send)

    def convolve(j, first, last):
        rows = slice(8 * j, 8 * j + 8)
        now = mx[1 + first : 1 + last, rows, :]
        window = jnp.concatenate([mx[first:last, rows, :], now], axis=2)
        window = window.reshape(8 * (last - first), 2 * taps).astype(jnp.bfloat16)
        conv = jnp.dot(window, toep[j], preferred_element_type=jnp.float32)
        direct = skip_b[j, pl.ds(x, 1)] * now
        gated = qb[first:last, rows, :] * (conv.reshape(last - first, 8, taps) + direct)
        return gated.astype(jnp.bfloat16)

    def out_copy(slab):
        at = CH[("out", 0)] + x
        return copy(("out", slab), send_out.at[slab], got.at[:, x], dev(y, zl, slab, h, c), at)

    def out_send(slab):
        @pl.when(x != slab)
        def _():
            out_copy(slab).start()

    for j in range(16):
        gated = convolve(j, 1, 2 * NX)
        for b in range(1, 2 * NX):
            send_out[b // 2, j, :, b % 2 * taps : (b % 2 + 1) * taps] = gated[b - 1]
    for slab in range(1, NX):
        out_send(slab)
    arrived(("edge",), edge_in)
    before_first = edge_in[...].astype(jnp.float32)
    mx[0] = jnp.where(g == 0, jnp.zeros_like(before_first), before_first)
    for j in range(16):
        send_out[0, j, :, 0:taps] = convolve(j, 0, 1)[0]
    out_send(0)
    got[:, x] = send_out[x]
    for k in range(1, NX):
        source = (x + NX - k) % NX
        arrived(("out", k), got.at[:, source], CH[("out", 0)] + source)
    out_ref[...] = got[...].astype(jnp.float32).reshape(out_ref.shape).astype(jnp.bfloat16)
    for slab in range(NX):
        @pl.when(x != slab)
        def _(slab=slab):
            out_copy(slab).wait_send()

    edge_copy().wait_send()
    all_sent()


def shards(tokens, norm_gain, in_weight, filter_taps, skip_gain):
    rows, din = tokens.shape
    taps = filter_taps.shape[1]
    wide = skip_gain.shape[0]
    count = len(CH)
    hbm = pl.BlockSpec(memory_space=pl.ANY)
    out = pl.pallas_call(
        kernel,
        out_shape=jax.ShapeDtypeStruct((wide, 4 * rows), jnp.bfloat16),
        in_specs=[hbm] * 5,
        out_specs=pl.BlockSpec(memory_space=pltpu.VMEM),
        scratch_shapes=[
            pltpu.VMEM((rows, din), jnp.bfloat16),
            pltpu.VMEM((1, din), jnp.float32),
            pltpu.VMEM(filter_taps.shape, jnp.float32),
            pltpu.VMEM((1, wide), jnp.float32),
            pltpu.VMEM((KC, 2, NX, 2, rows, din // KC), jnp.bfloat16),
            pltpu.VMEM((NY * NZ, 2, 8, din), jnp.bfloat16),
            pltpu.VMEM((8 * NY * NZ, NX * 2 * rows), jnp.float32),
            pltpu.VMEM((16, 2 * taps, taps), jnp.bfloat16),
            pltpu.VMEM((16, NX, 8, 128), jnp.float32),
            pltpu.VMEM((2 * NX, 128, 2 * rows), jnp.float32),
            pltpu.VMEM((2 * NX + 1, 128, 2 * rows), jnp.float32),
            pltpu.VMEM((128, 2 * rows), jnp.bfloat16),
            pltpu.VMEM((128, 2 * rows), jnp.bfloat16),
            pltpu.VMEM((NX, 16, 8, 4 * rows), jnp.bfloat16),
            pltpu.VMEM((16, NX, 8, 4 * rows), jnp.bfloat16),
            pltpu.SemaphoreType.DMA((count,)),
            pltpu.SemaphoreType.DMA((count,)),
            pltpu.SemaphoreType.DMA((5,)),
            pltpu.SemaphoreType.REGULAR,
        ],
        compiler_params=pltpu.CompilerParams(
            collective_id=0, has_side_effects=True, vmem_limit_bytes=56 * 2**20
        ),
    )(tokens, norm_gain.reshape(1, din), in_weight.T, filter_taps, skip_gain.reshape(1, wide))
    return out.T


def solution(mesh):
    return jax.shard_map(
        shards,
        mesh=mesh,
        in_specs=(P(("fsdp", "tp"), None), P(), P(None, ("fsdp", "tp")), P("tp", None), P("tp")),
        out_specs=P("fsdp", "tp"),
        check_vma=False,
    )
```

time: 1490 us -> 69.3 us (0.05)
  the two profiles are of different devices: /device:TPU:2 before, /device:TPU:1 now
where the time goes in v2:
time: 69.3 us; the launch traced here: 69.1 us
  Pallas kernels  67.3 us (97%)
  local copies, waits for them, and re-layouts  1.8 us (3%)
    pallas_call x1, Pallas kernels, shards(): pl.pallas_call(kernel, out_shape=jax.ShapeDtypeStruct((wide, 4 * rows), j...  67.3 us
    transpose x1, local copies, waits for them, and re-layouts, shards(): return out.T  1.8 us

profile of v2, /device:TPU:1, one launch (start us, length us, event | category | flops | bytes accessed | tf_op | source)
XLA Modules:
  0.0 69.1 jit_solution(15618764378967482226)
XLA Ops:
  0.0 67.3 %shard_map.55 = bf16[512,256]{1,0:T(8,128)(2,1)} custom-call(bf16[64,2048]{1,0:T(8,128)(2,1)} %tokens_hbm.1, f32[1,2048]{1,0:T(1,128)} %bitcast.6, bf16[8,2048]{1,0:T(8,128)(2,1)} %bitcast.5, f32[32,128]{1,0:T(8,128)} %taps_hbm.1, f32[1,512]{1,0:T(1,128)} %bitcast.7), custom_call_target="tpu_custom_call" | custom-call | tf_op jit(solution)/shard_map/pallas_call | solution.py:374
  67.3 1.8 %copy.6 = bf16[256,512]{1,0:T(8,128)(2,1)} copy(bf16[256,512]{0,1:T(8,128)(2,1)} %bitcast.4) | data formatting | bytes 524288 | tf_op jit(solution)/shard_map/transpose | solution.py:404

commit v3 on v2

--- a/solution.py
+++ b/solution.py
@@ -11,7 +11,8 @@
 NX, NY, NZ = 4, 8, 6
 KC = 8
 Y_DEPTH = 4
-CROSS_DEPTH = 2
+EARLY_DEPTH = 1
+LATE_DEPTH = 4
 GROUP = 2
 OWN_AT = 7
 OX_AT = 2
@@ -46,7 +47,7 @@
 def kernel(
     tokens_hbm, gain_hbm, w_hbm, taps_hbm, skip_hbm, out_ref,
     tokens_ref, gain_ref, taps_ref, skip_ref,
-    tb, wb, acc, toep, skip_b, qb, mx, edge_out, edge_in, send_out, got, ssem, rsem, lsem, ready,
+    tb, wb, acc, toep, skip_b, qb, mx, edge_out, edge_in, send_out, ssem, rsem, lsem, ready,
 ):
     f = lax.axis_index("fsdp")
     t = lax.axis_index("tp")
@@ -238,10 +239,18 @@
             arrived(("ox", k), piece)
             send(("os", k), piece, piece, sibling)
 
-        def cross(kc):
-            if kc >= CROSS_DEPTH:
-                sent(("cr", kc - CROSS_DEPTH))
-            send(("cr", kc), tb.at[kc, 0, x], tb.at[kc, 1, x], partner)
+        def cross_copy(kc):
+            return copy(("cr", kc), tb.at[kc, 0, x], tb.at[kc, 1, x], partner)
+
+        depths = ((0, EARLY_DEPTH), (1, LATE_DEPTH))
+
+        def cross_next(kc):
+            for half, depth in depths:
+                @pl.when(h == half)
+                def _(depth=depth):
+                    cross_copy(kc).wait_send()
+                    if kc + depth < KC:
+                        cross_copy(kc + depth).start()
 
         def on_cr(kc):
             piece = far_piece(kc, 0)
@@ -264,12 +273,15 @@
             pl.semaphore_wait(ready, 1)
 
         tables()
-        for kc in range(CROSS_DEPTH):
-            cross(kc)
+        for half, depth in depths:
+            @pl.when(h == half)
+            def _(depth=depth):
+                for kc in range(depth):
+                    cross_copy(kc).start()
+
         for kc in range(KC):
             on_cr(kc)
-            if kc + CROSS_DEPTH < KC:
-                cross(kc + CROSS_DEPTH)
+            cross_next(kc)
             if kc >= 1:
                 for k in (1, 3, 2):
                     on_cx(kc - 1, k)
@@ -332,7 +344,7 @@
 
     def out_copy(slab):
         at = CH[("out", 0)] + x
-        return copy(("out", slab), send_out.at[slab], got.at[:, x], dev(y, zl, slab, h, c), at)
+        return copy(("out", slab), send_out.at[slab], out_ref.at[:, x], dev(y, zl, slab, h, c), at)
 
     def out_send(slab):
         @pl.when(x != slab)
@@ -351,11 +363,12 @@
     for j in range(16):
         send_out[0, j, :, 0:taps] = convolve(j, 0, 1)[0]
     out_send(0)
-    got[:, x] = send_out[x]
+    own_out = pltpu.make_async_copy(send_out.at[x], out_ref.at[:, x], lsem.at[0])
+    own_out.start()
     for k in range(1, NX):
         source = (x + NX - k) % NX
-        arrived(("out", k), got.at[:, source], CH[("out", 0)] + source)
-    out_ref[...] = got[...].astype(jnp.float32).reshape(out_ref.shape).astype(jnp.bfloat16)
+        arrived(("out", k), out_ref.at[:, source], CH[("out", 0)] + source)
+    own_out.wait()
     for slab in range(NX):
         @pl.when(x != slab)
         def _(slab=slab):
@@ -373,9 +386,9 @@
     hbm = pl.BlockSpec(memory_space=pl.ANY)
     out = pl.pallas_call(
         kernel,
-        out_shape=jax.ShapeDtypeStruct((wide, 4 * rows), jnp.bfloat16),
+        out_shape=jax.ShapeDtypeStruct((16, NX, 8, 4 * rows), jnp.bfloat16),
         in_specs=[hbm] * 5,
-        out_specs=pl.BlockSpec(memory_space=pltpu.VMEM),
+        out_specs=hbm,
         scratch_shapes=[
             pltpu.VMEM((rows, din), jnp.bfloat16),
             pltpu.VMEM((1, din), jnp.float32),
@@ -391,7 +404,6 @@
             pltpu.VMEM((128, 2 * rows), jnp.bfloat16),
             pltpu.VMEM((128, 2 * rows), jnp.bfloat16),
             pltpu.VMEM((NX, 16, 8, 4 * rows), jnp.bfloat16),
-            pltpu.VMEM((16, NX, 8, 4 * rows), jnp.bfloat16),
             pltpu.SemaphoreType.DMA((count,)),
             pltpu.SemaphoreType.DMA((count,)),
             pltpu.SemaphoreType.DMA((5,)),
@@ -401,7 +413,7 @@
             collective_id=0, has_side_effects=True, vmem_limit_bytes=56 * 2**20
         ),
     )(tokens, norm_gain.reshape(1, din), in_weight.T, filter_taps, skip_gain.reshape(1, wide))
-    return out.T
+    return out.reshape(wide, 4 * rows).T
 
 
 def solution(mesh):

time: 69.3 us -> 66.7 us (0.962)
  Pallas kernels: 67.3 us -> 64.7 us
    pallas_call x1, Pallas kernels: 67.3 us -> 64.7 us  [shards(): pl.pallas_call(kernel, out_shape=jax.ShapeDtypeStruct((16, NX, 8, 4 * row...]
    transpose x1 -> x0, local copies, waits for them, and re-layouts: 1.8 us -> none  [shards(): return out.T]
    reshape x0 -> x1, local copies, waits for them, and re-layouts: none -> 1.8 us  [shards(): return out.reshape(wide, 4 * rows).T]
where the time goes in v3:
time: 66.7 us; the launch traced here: 66.5 us
  Pallas kernels  64.7 us (97%)
  local copies, waits for them, and re-layouts  1.8 us (3%)
    pallas_call x1, Pallas kernels, shards(): pl.pallas_call(kernel, out_shape=jax.ShapeDtypeStruct((16, NX, 8, 4 * row...  64.7 us
    reshape x1, local copies, waits for them, and re-layouts, shards(): return out.reshape(wide, 4 * rows).T  1.8 us

profile of v3, /device:TPU:1, one launch (start us, length us, event | category | flops | bytes accessed | tf_op | source)
XLA Modules:
  0.0 66.5 jit_solution(17387122556864456790)
XLA Ops:
  0.0 64.7 %shard_map.55 = bf16[16,4,8,256]{3,2,1,0:T(8,128)(2,1)} custom-call(bf16[64,2048]{1,0:T(8,128)(2,1)} %tokens_hbm.1, f32[1,2048]{1,0:T(1,128)} %bitcast.7, bf16[8,2048]{1,0:T(8,128)(2,1)} %bitcast.6, f32[32,128]{1,0:T(8,128)} %taps_hbm.1, f32[1,512]{1,0:T(1,128)} %bitcast.8), custom_call_target="tpu_custom_call" | custom-call | tf_op jit(solution)/shard_map/pallas_call | solution.py:387
  64.7 1.8 %copy.6 = bf16[512,256]{0,1:T(8,128)(2,1)} copy(bf16[512,256]{1,0:T(8,128)(2,1)} %bitcast.5) | data formatting | bytes 524288 | tf_op jit(solution)/shard_map/reshape | solution.py:416
